TPU v7x, 128 devices: a whole 4x4x4 slice. The times are simulated.
128 devices in a mesh: grp: 4 (over y_lo, core), dev: 32 (over y_hi, z, x).
Axes of the slice: x: 4, y: 4 (y_hi: 2, y_lo: 2; y = y_hi * 2 + y_lo), z: 4, core: 2. Of those that a mesh axis runs over, the one named last changes fastest.
Arguments:
- queries: bfloat16 [65536, 4096], P(('grp', 'dev')), may hold values from -0.3125 to 0.3125
- documents: bfloat16 [65536, 4096], P(('grp', 'dev')), may hold values from -0.3125 to 0.3125
- pair_index: int32 [128, 512], P(('grp', 'dev')), may hold values from 0 to 511, each once within a row
Outputs:
- query_grad: bfloat16 [65536, 4096], P(('grp', 'dev'))
- doc_grad: bfloat16 [65536, 4096], P(('grp', 'dev'))
- row_loss: float32 [65536], P(('grp', 'dev'))
- column_loss: float32 [65536], P(('grp', 'dev'))
Inputs may be any that keep to these rules, and one draw needn't show every extreme that they name: Each row of pair_index is a permutation of 0 to 511: query r of block b pairs with document b * 512 + pair_index[b, r].
All inputs are finite; a program needn't handle non-finite values.
Results may differ from a plain program's by a relative error of at most 0.0034.
Values may be sent and summed in bfloat16 or wider, within the bound.
A program may use at most 128 MiB of HBM per device.

v0:
```python
from functools import reduce

import jax
import jax.numpy as jnp
from jax import lax
from jax.sharding import PartitionSpec as P

logit_scale = 20.0


def swapped(block, axis, distance):
    count = lax.axis_size(axis)
    route = []
    for low in range(count):
        high = low | 1 << distance
        if high != low and high < count:
            route += [(low, high), (high, low)]
    return lax.ppermute(block, axis, route)


def tile_of(left_rows, right_rows):
    return logit_scale * lax.dot_general(
        left_rows, right_rows, (((1,), (1,)), ((), ())), preferred_element_type=jnp.float32
    )


def apply_left(weights, right_rows):
    return jnp.dot(weights, right_rows, preferred_element_type=jnp.float32)


def apply_transposed(weights, left_rows):
    return lax.dot_general(
        weights, left_rows, (((0,), (0,)), ((), ())), preferred_element_type=jnp.float32
    )


def row_lse_of(tile_list):
    maximum = reduce(jnp.maximum, [jnp.max(member, axis=1) for member in tile_list])
    totals = reduce(
        jnp.add, [jnp.sum(jnp.exp(member - maximum[:, None]), axis=1) for member in tile_list]
    )
    return maximum + jnp.log(totals)


def column_partial(tile_now):
    maximum = jnp.max(tile_now, axis=0)
    return (maximum, jnp.sum(jnp.exp(tile_now - maximum[None, :]), axis=0))


def merge_partials(partial_list):
    maximum = reduce(jnp.maximum, [member[0] for member in partial_list])
    totals = reduce(jnp.add, [member[1] * jnp.exp(member[0] - maximum) for member in partial_list])
    return maximum + jnp.log(totals)


def grad_tile(tile_now, row_stat, column_stat):
    return jnp.exp(tile_now - row_stat[:, None]) + jnp.exp(tile_now - column_stat[None, :])


def shards(queries, documents, pair_index):
    row_count = queries.shape[0]
    dev_count = lax.axis_size("dev")
    partner_bits = (dev_count.bit_length() - 1, dev_count.bit_length() - 2)
    onehot = (pair_index[0][:, None] == jnp.arange(row_count, dtype=jnp.int32)[None, :]).astype(
        jnp.float32
    )
    self_tile = tile_of(queries, documents)
    query_sum = jnp.zeros(queries.shape, jnp.float32)
    doc_sum = jnp.zeros(documents.shape, jnp.float32)
    partner_docs = [swapped(documents, ("grp", "dev"), swap_bit) for swap_bit in partner_bits]
    row_tiles = [tile_of(queries, far_docs) for far_docs in partner_docs]
    row_lse = row_lse_of([self_tile] + row_tiles)
    returned = []
    for far_tile, swap_bit in zip(row_tiles, partner_bits):
        maximum, totals = column_partial(far_tile)
        returned.append(swapped((maximum, totals), ("grp", "dev"), swap_bit))
    column_lse = merge_partials([column_partial(self_tile)] + returned)
    far_columns = [swapped(column_lse, ("grp", "dev"), swap_bit) for swap_bit in partner_bits]
    for far_tile, far_docs, far_lse, swap_bit in zip(
        row_tiles, partner_docs, far_columns, partner_bits
    ):
        weights = grad_tile(far_tile, row_lse, far_lse).astype(jnp.bfloat16)
        query_sum = query_sum + apply_left(weights, far_docs)
        share = apply_transposed(weights, queries).astype(jnp.bfloat16)
        doc_sum = doc_sum + swapped(share, ("grp", "dev"), swap_bit).astype(jnp.float32)
    self_grad = (grad_tile(self_tile, row_lse, column_lse) - 2.0 * onehot).astype(jnp.bfloat16)
    query_sum = query_sum + apply_left(self_grad, documents)
    doc_sum = doc_sum + apply_transposed(self_grad, queries)
    positive_rows = jnp.sum(onehot * self_tile, axis=1)
    positive_columns = jnp.sum(onehot * self_tile, axis=0)
    return (
        (logit_scale * query_sum).astype(jnp.bfloat16),
        (logit_scale * doc_sum).astype(jnp.bfloat16),
        row_lse - positive_rows,
        column_lse - positive_columns,
    )


def solution(mesh):
    return jax.shard_map(
        shards,
        mesh=mesh,
        in_specs=(P(("grp", "dev"), None), P(("grp", "dev"), None), P(("grp", "dev"), None)),
        out_specs=(
            P(("grp", "dev"), None),
            P(("grp", "dev"), None),
            P(("grp", "dev")),
            P(("grp", "dev")),
        ),
        check_vma=False,
    )
```

profile of v0, /device:TPU:1, one launch (start us, length us, event | category | flops | bytes accessed | tf_op | source)
XLA Modules:
  0.0 215.8 jit_solution(7675287329189289162)
XLA Ops:
  0.6 3.8 %collective-permute-start.1 = (bf16[512,4096]{1,0:T(8,128)(2,1)}, bf16[512,4096]{1,0:T(8,128)(2,1)S(1)}, u32[]{:S(2)}, u32[]{:S(2)}) collective-permute-start(bf16[512,4096]{1,0:T(8,128)(2,1)} %param.4), channel_id=1, source_target_pairs={{0,16},{16,0},{1,17},{17,1},{2,18},{18,2},{3,19},{19,3},{4,20},{20... | collective-permute-start | bytes 12582920 | tf_op jit(solution)/shard_map/ppermute | solution.py:18
  4.5 1.0 collective-permute-start
  5.4 5.9 %fusion.7 = (f32[512]{0:T(512)S(1)}, f32[512]{0:T(512)S(1)}, f32[512,512]{1,0:T(8,128)S(1)}) fusion(bf16[512,4096]{1,0:T(8,128)(2,1)} %param.3, bf16[512,4096]{1,0:T(8,128)(2,1)} %param.4), kind=kOutput, calls=%fused_computation.27 | convolution fusion | flops 2148269056 | bytes 9441280 | tf_op jit(solution)/shard_map/dot_general | solution.py:22
  11.3 83.4 %collective-permute-done.1 = bf16[512,4096]{1,0:T(8,128)(2,1)S(1)} collective-permute-done((bf16[512,4096]{1,0:T(8,128)(2,1)}, bf16[512,4096]{1,0:T(8,128)(2,1)S(1)}, u32[]{:S(2)}, u32[]{:S(2)}) %collective-permute-start.1) | collective-permute-done | bytes 4194336 | tf_op jit(solution)/shard_map/ppermute | solution.py:18
  94.7 2.7 %fusion.8 = (f32[512]{0:T(512)S(1)}, f32[512]{0:T(512)S(1)}, f32[512,512]{1,0:T(8,128)S(1)}) fusion(bf16[512,4096]{1,0:T(8,128)(2,1)S(1)} %copy-done, bf16[512,4096]{1,0:T(8,128)(2,1)S(1)} %collective-permute-done.1), kind=kOutput, calls=%fused_computation.28 | convolution fusion | flops 2148269056 | bytes 9441280 | tf_op jit(solution)/shard_map/dot_general | solution.py:22
  97.4 3.0 %collective-permute-start.3 = (f32[512]{0:T(512)S(1)}, f32[512]{0:T(512)S(1)}, u32[]{:S(2)}, u32[]{:S(2)}) collective-permute-start(f32[512]{0:T(512)S(1)} %get-tuple-element.17), channel_id=1, source_target_pairs={{0,16},{16,0},{1,17},{17,1},{2,18},{18,2},{3,19},{19,3},{4,20},{20... | collective-permute-start | bytes 6152 | tf_op jit(solution)/shard_map/ppermute | solution.py:18
  100.4 0.0 collective-permute-done
  100.4 2.7 %fusion.6 = (f32[512]{0:T(512)S(1)}, f32[512]{0:T(512)S(1)}, f32[512,512]{1,0:T(8,128)S(1)}) fusion(bf16[512,4096]{1,0:T(8,128)(2,1)S(1)} %copy-done, bf16[512,4096]{1,0:T(8,128)(2,1)S(1)} %collective-permute-done), kind=kOutput, calls=%fused_computation.26 | convolution fusion | flops 2148269056 | bytes 9441280 | tf_op jit(solution)/shard_map/dot_general | solution.py:22
  103.1 1.2 fusion.1
  104.3 0.1 collective-permute-start.5
  104.4 2.1 collective-permute-start.4
  106.5 0.0 collective-permute-start.2
  106.5 1.8 collective-permute-done.5
  108.3 0.0 collective-permute-done.3
  108.3 0.0 collective-permute-done.4
  108.3 0.0 collective-permute-done.2
  108.3 0.6 fusion.9
  108.9 2.3 %collective-permute-start.7 = (f32[512]{0:T(512)S(1)}, f32[512]{0:T(512)S(1)}, u32[]{:S(2)}, u32[]{:S(2)}) collective-permute-start(f32[512]{0:T(512)S(1)} %get-tuple-element.23), channel_id=1, source_target_pairs={{0,16},{16,0},{1,17},{17,1},{2,18},{18,2},{3,19},{19,3},{4,20},{20... | collective-permute-start | bytes 6152 | tf_op jit(solution)/shard_map/ppermute | solution.py:18
  111.2 0.6 fusion.10
  111.8 1.0 collective-permute-start.6
  112.8 0.1 collective-permute-done.7
  112.8 2.5 %convolution_convert_fusion = bf16[512,4096]{1,0:T(8,128)(2,1)S(1)} fusion(bf16[512,4096]{1,0:T(8,128)(2,1)S(1)} %copy-done, f32[512,512]{1,0:T(8,128)S(1)} %get-tuple-element.27, f32[512]{0:T(512)S(1)} %collective-permute-done.7, f32[512]{0:T(512)S(1)} %get-tuple-element.25), kind=kOutput, calls=%fused_computation.2 | convolution fusion | flops 2150629376 | bytes 9441280 | tf_op jit(solution)/shard_map/dot_general | solution.py:32
  115.4 0.0 copy-start.3
  115.4 3.0 %collective-permute-start.9 = (bf16[512,4096]{1,0:T(8,128)(2,1)S(1)}, bf16[512,4096]{1,0:T(8,128)(2,1)}, u32[]{:S(2)}, u32[]{:S(2)}) collective-permute-start(bf16[512,4096]{1,0:T(8,128)(2,1)S(1)} %convolution_convert_fusion), channel_id=1, source_target_pairs={{0,16},{16,0},{1,17},{17,1},{2,18},{18,2},{3,19},{19,3},{4,20},{20... | collective-permute-start | bytes 12582920 | tf_op jit(solution)/shard_map/ppermute | solution.py:18
  118.4 0.0 collective-permute-done.6
  118.4 4.5 %convolution_convert_fusion.1 = bf16[512,4096]{1,0:T(8,128)(2,1)} fusion(bf16[512,4096]{1,0:T(8,128)(2,1)S(1)} %copy-done, f32[512,512]{1,0:T(8,128)S(1)} %get-tuple-element.28, f32[512]{0:T(512)S(1)} %collective-permute-done.6, f32[512]{0:T(512)S(1)} %get-tuple-element.25), kind=kOutput, calls=%fused_computation.3 | convolution fusion | flops 2150629376 | bytes 9441280 | tf_op jit(solution)/shard_map/dot_general | solution.py:32
  122.8 1.5 collective-permute-start.8
  124.4 5.8 %fusion.5 = f32[512,4096]{1,0:T(8,128)} fusion(bf16[512,4096]{1,0:T(8,128)(2,1)S(1)} %copy-done.3, f32[512,512]{1,0:T(8,128)S(1)} %get-tuple-element.26, s32[512]{0:T(512)S(1)} %bitcast.14, f32[512]{0:T(512)S(1)} %get-tuple-element.23, f32[512]{0:T(512)S(1)} %get-tuple-element.25), kind=kOutput, calls=%fused_computation.25 | convolution fusion | flops 2149318656 | bytes 13637632 | tf_op jit(solution)/shard_map/dot_general | solution.py:28
  130.2 2.5 %fusion.3 = f32[512,4096]{1,0:T(8,128)S(1)} fusion(bf16[512,4096]{1,0:T(8,128)(2,1)S(1)} %collective-permute-done.1, f32[512,512]{1,0:T(8,128)S(1)} %get-tuple-element.27, f32[512]{0:T(512)S(1)} %collective-permute-done.7, f32[512]{0:T(512)S(1)} %get-tuple-element.25), kind=kOutput, calls=%fused_computation.23 | convolution fusion | flops 2148532224 | bytes 13635584 | tf_op jit(solution)/shard_map/dot_general | solution.py:28
  132.6 8.1 %multiply_convert_fusion.1 = bf16[512,4096]{1,0:T(8,128)(2,1)} fusion(f32[512,4096]{1,0:T(8,128)} %fusion.5, f32[512,4096]{1,0:T(8,128)S(1)} %fusion.3, bf16[512,4096]{1,0:T(8,128)(2,1)} %copy-done.1, f32[512,512]{1,0:T(8,128)S(1)} %get-tuple-element.28, f32[512]{0:T(512)S(1)} %collective-permute-done.6, f32[512]{0:T(512)S(1)} %get-tuple-element.25), kind=kOutput, calls=%fused_computation.1 | convolution fusion | flops 2156920832 | bytes 26218496 | tf_op jit(solution)/shard_map/dot_general | solution.py:28
  140.7 66.2 %collective-permute-done.9 = bf16[512,4096]{1,0:T(8,128)(2,1)} collective-permute-done((bf16[512,4096]{1,0:T(8,128)(2,1)S(1)}, bf16[512,4096]{1,0:T(8,128)(2,1)}, u32[]{:S(2)}, u32[]{:S(2)}) %collective-permute-start.9) | collective-permute-done | bytes 4194336 | tf_op jit(solution)/shard_map/ppermute | solution.py:18
  207.0 8.9 %multiply_convert_fusion = bf16[512,4096]{1,0:T(8,128)(2,1)} fusion(bf16[512,4096]{1,0:T(8,128)(2,1)} %collective-permute-done.9, bf16[512,4096]{1,0:T(8,128)(2,1)} %collective-permute-done.8, bf16[512,4096]{1,0:T(8,128)(2,1)S(1)} %copy-done, f32[512,512]{1,0:T(8,128)S(1)} %get-tuple-element.26, s32[512]{0:T(512)S(1)} %bitcast.15, ...), kind=kOutput, calls=%fused_computation | convolution fusion | flops 2161901568 | bytes 17831936 | tf_op jit(solution)/shard_map/dot_general | solution.py:32
  (9 shorter events, 0.0 us)
Async XLA Ops:
  0.6 94.1 %copy-start = (bf16[512,4096]{1,0:T(8,128)(2,1)S(1)}, bf16[512,4096]{1,0:T(8,128)(2,1)}, u32[]{:S(2)}) copy-start(bf16[512,4096]{1,0:T(8,128)(2,1)} %param.3) | copy-start | bytes 12582916
  0.6 94.1 %collective-permute-start.1 = (bf16[512,4096]{1,0:T(8,128)(2,1)}, bf16[512,4096]{1,0:T(8,128)(2,1)S(1)}, u32[]{:S(2)}, u32[]{:S(2)}) collective-permute-start(bf16[512,4096]{1,0:T(8,128)(2,1)} %param.4), channel_id=1, source_target_pairs={{0,16},{16,0},{1,17},{17,1},{2,18},{18,2},{3,19},{19,3},{4,20},{20... | collective-permute-start | bytes 12582920 | tf_op jit(solution)/shard_map/ppermute | solution.py:18
  4.5 95.9 %collective-permute-start = (bf16[512,4096]{1,0:T(8,128)(2,1)}, bf16[512,4096]{1,0:T(8,128)(2,1)S(1)}, u32[]{:S(2)}, u32[]{:S(2)}) collective-permute-start(bf16[512,4096]{1,0:T(8,128)(2,1)} %param.4), channel_id=1, source_target_pairs={{0,32},{32,0},{1,33},{33,1},{2,34},{34,2},{3,35},{35,3},{4,36},{36... | collective-permute-start | bytes 12582920 | tf_op jit(solution)/shard_map/ppermute | solution.py:18
  97.4 5.7 %copy-start.2 = (s32[1,512]{1,0:T(1,128)S(1)}, s32[1,512]{1,0:T(1,128)}, u32[]{:S(2)}) copy-start(s32[1,512]{1,0:T(1,128)} %param.5) | copy-start | bytes 6148
  97.4 10.9 %collective-permute-start.3 = (f32[512]{0:T(512)S(1)}, f32[512]{0:T(512)S(1)}, u32[]{:S(2)}, u32[]{:S(2)}) collective-permute-start(f32[512]{0:T(512)S(1)} %get-tuple-element.17), channel_id=1, source_target_pairs={{0,16},{16,0},{1,17},{17,1},{2,18},{18,2},{3,19},{19,3},{4,20},{20... | collective-permute-start | bytes 6152 | tf_op jit(solution)/shard_map/ppermute | solution.py:18
  100.4 15.0 %copy-start.1 = (bf16[512,4096]{1,0:T(8,128)(2,1)}, bf16[512,4096]{1,0:T(8,128)(2,1)S(1)}, u32[]{:S(2)}) copy-start(bf16[512,4096]{1,0:T(8,128)(2,1)S(1)} %collective-permute-done) | copy-start | bytes 12582916
  104.3 4.0 %collective-permute-start.5 = (f32[512]{0:T(512)S(1)}, f32[512]{0:T(512)S(1)}, u32[]{:S(2)}, u32[]{:S(2)}) collective-permute-start(f32[512]{0:T(512)S(1)} %get-tuple-element.20), channel_id=1, source_target_pairs={{0,16},{16,0},{1,17},{17,1},{2,18},{18,2},{3,19},{19,3},{4,20},{20... | collective-permute-start | bytes 6152 | tf_op jit(solution)/shard_map/ppermute | solution.py:18
  104.4 3.9 %collective-permute-start.4 = (f32[512]{0:T(512)S(1)}, f32[512]{0:T(512)S(1)}, u32[]{:S(2)}, u32[]{:S(2)}) collective-permute-start(f32[512]{0:T(512)S(1)} %get-tuple-element.18), channel_id=1, source_target_pairs={{0,32},{32,0},{1,33},{33,1},{2,34},{34,2},{3,35},{35,3},{4,36},{36... | collective-permute-start | bytes 6152 | tf_op jit(solution)/shard_map/ppermute | solution.py:18
  106.5 1.8 collective-permute-start.2
  108.9 3.9 %collective-permute-start.7 = (f32[512]{0:T(512)S(1)}, f32[512]{0:T(512)S(1)}, u32[]{:S(2)}, u32[]{:S(2)}) collective-permute-start(f32[512]{0:T(512)S(1)} %get-tuple-element.23), channel_id=1, source_target_pairs={{0,16},{16,0},{1,17},{17,1},{2,18},{18,2},{3,19},{19,3},{4,20},{20... | collective-permute-start | bytes 6152 | tf_op jit(solution)/shard_map/ppermute | solution.py:18
  111.8 6.6 %collective-permute-start.6 = (f32[512]{0:T(512)S(1)}, f32[512]{0:T(512)S(1)}, u32[]{:S(2)}, u32[]{:S(2)}) collective-permute-start(f32[512]{0:T(512)S(1)} %get-tuple-element.23), channel_id=1, source_target_pairs={{0,32},{32,0},{1,33},{33,1},{2,34},{34,2},{3,35},{35,3},{4,36},{36... | collective-permute-start | bytes 6152 | tf_op jit(solution)/shard_map/ppermute | solution.py:18
  115.4 9.0 %copy-start.3 = (bf16[512,4096]{1,0:T(8,128)(2,1)S(1)}, bf16[512,4096]{1,0:T(8,128)(2,1)}, u32[]{:S(2)}) copy-start(bf16[512,4096]{1,0:T(8,128)(2,1)} %param.4) | copy-start | bytes 12582916
  115.4 91.6 %collective-permute-start.9 = (bf16[512,4096]{1,0:T(8,128)(2,1)S(1)}, bf16[512,4096]{1,0:T(8,128)(2,1)}, u32[]{:S(2)}, u32[]{:S(2)}) collective-permute-start(bf16[512,4096]{1,0:T(8,128)(2,1)S(1)} %convolution_convert_fusion), channel_id=1, source_target_pairs={{0,16},{16,0},{1,17},{17,1},{2,18},{18,2},{3,19},{19,3},{4,20},{20... | collective-permute-start | bytes 12582920 | tf_op jit(solution)/shard_map/ppermute | solution.py:18
  122.8 84.1 %collective-permute-start.8 = (bf16[512,4096]{1,0:T(8,128)(2,1)}, bf16[512,4096]{1,0:T(8,128)(2,1)}, u32[]{:S(2)}, u32[]{:S(2)}) collective-permute-start(bf16[512,4096]{1,0:T(8,128)(2,1)} %convolution_convert_fusion.1), channel_id=1, source_target_pairs={{0,32},{32,0},{1,33},{33,1},{2,34},{34,2},{3,35},{35,3},{4,36},{36... | collective-permute-start | bytes 12582920 | tf_op jit(solution)/shard_map/ppermute | solution.py:18
where the time goes:
time: 218 us; the launch traced here: 216 us
  waiting for transfers between devices  152 us (70%)
  matrix products  43.5 us (20%)
  starting transfers between devices  17.7 us (8%)
  other arithmetic  2.39 us (1%)
    ppermute x10, waiting for transfers between devices, swapped(): return lax.ppermute(block, axis, route)  152 us
    ppermute x10, starting transfers between devices, swapped(): return lax.ppermute(block, axis, route)  17.7 us
    dot_general x3, matrix products, apply_left(): return jnp.dot(weights, right_rows, preferred_element_type=jnp.float32)  16.4 us
    dot_general x3, matrix products, apply_transposed(): lax.dot_general(weights, left_rows, (((0,), (0,)), ((), ())), preferred_e...  15.9 us
    dot_general x3, matrix products, tile_of(): lax.dot_general(left_rows, right_rows, (((1,), (1,)), ((), ())), preferre...  11.3 us
  transfers between devices with their start and end apart: 10, of which 4 were waited for; matrix products, arithmetic and copies ran while one was open for 17% of the time, Pallas kernels for 0%

commit v1 on v0

v1 whole, which is shorter than its diff:
```python
import jax
import jax.numpy as jnp
from jax import lax
from jax.experimental import pallas as pl
from jax.experimental.pallas import tpu as pltpu
from jax.sharding import PartitionSpec as P

logit_scale = 20.0
MESH = pl.DeviceIdType.MESH
ROWS = 512
D = 4096
K_CHUNK = 128
K_COUNT = ROWS // K_CHUNK
P_CHUNK = 64
P_COUNT = ROWS // P_CHUNK
WIDE = 512


def tile_into(out, left, right, first, count, step):
    @pl.loop(0, count)
    def _(i):
        at = pl.multiple_of(first + i * step, step)
        out[:, pl.ds(at, step)] = logit_scale * lax.dot_general(
            left[...],
            right[pl.ds(at, step), :],
            (((1,), (1,)), ((), ())),
            preferred_element_type=jnp.float32,
        )


def dot(a, b):
    return jnp.dot(a, b, preferred_element_type=jnp.float32)


def column_partial(tiles):
    top = tiles[0][...].max(axis=0, keepdims=True)
    for t in tiles[1:]:
        top = jnp.maximum(top, t[...].max(axis=0, keepdims=True))
    total = jnp.exp(tiles[0][...] - top).sum(axis=0, keepdims=True)
    for t in tiles[1:]:
        total = total + jnp.exp(t[...] - top).sum(axis=0, keepdims=True)
    return top, total


def row_partial(tiles):
    top = tiles[0][...].max(axis=1, keepdims=True)
    for t in tiles[1:]:
        top = jnp.maximum(top, t[...].max(axis=1, keepdims=True))
    total = jnp.exp(tiles[0][...] - top).sum(axis=1, keepdims=True)
    for t in tiles[1:]:
        total = total + jnp.exp(t[...] - top).sum(axis=1, keepdims=True)
    return top, total


def exchange(
    q_hbm, k_hbm, pair_ref, dq, dk, loss,
    q, k, q_core, k_core, k_far, share_out, share_in, acc,
    s_own, s_right, s_left, s_far,
    g_own, g_right, g_far, gt_own, gt_left, gt_far,
    row_top, row_sum, row_out, row_in, part_out, part_in,
    back_out, back_in, col_out, col_in,
    local_sem, doc_send, doc_recv, core_send, core_recv, stat_send, stat_recv,
    share_send, share_recv,
):
    g = lax.axis_index("grp")
    d = lax.axis_index("dev")
    core = lax.rem(g, 2)
    half = lax.axis_size("dev") // 2
    core_partner = (g + 1 - 2 * core, d)
    far_partner = (g, lax.rem(d + half, 2 * half))

    barrier = pltpu.get_barrier_semaphore()
    for other in (core_partner, far_partner):
        pl.semaphore_signal(barrier, inc=1, device_id=other, device_id_type=MESH)
    pl.semaphore_wait(barrier, 2)

    def remote(src, dst, send, recv, to):
        return pltpu.make_async_remote_copy(
            src_ref=src, dst_ref=dst, send_sem=send, recv_sem=recv,
            device_id=to, device_id_type=MESH,
        )

    def doc_copy(i):
        rows = pl.ds(i * K_CHUNK, K_CHUNK)
        return remote(k_hbm.at[rows], k_far.at[rows], doc_send.at[i], doc_recv.at[i], far_partner)

    def share_copy(i):
        rows = pl.ds(pl.multiple_of(i * P_CHUNK, P_CHUNK), P_CHUNK)
        return remote(
            share_out.at[rows], share_in.at[rows], share_send.at[i], share_recv.at[i], far_partner
        )

    @pl.when(core == 0)
    def _():
        for i in range(K_COUNT):
            doc_copy(i).start()

    k_move = remote(k_hbm, k_core, core_send.at[0], core_recv.at[0], core_partner)
    q_move = remote(q_hbm, q_core, core_send.at[1], core_recv.at[1], core_partner)
    q_load = pltpu.make_async_copy(q_hbm, q, local_sem.at[0])
    k_load = pltpu.make_async_copy(k_hbm, k, local_sem.at[1])
    q_load.start()
    k_load.start()
    k_move.start()
    q_move.start()
    q_load.wait()
    k_load.wait()
    tile_into(s_own, q, k, 0, 2, 256)
    k_move.wait_recv()
    tile_into(s_right, q, k_core, 0, 2, 256)
    q_move.wait_recv()
    tile_into(s_left, q_core, k, 0, 2, 256)

    top, total = column_partial([s_own, s_left])
    part_out[0:1, :] = top
    part_out[1:2, :] = total
    part_move = remote(part_out, part_in, stat_send.at[0], stat_recv.at[0], far_partner)
    part_move.start()

    @pl.when(core == 1)
    def _():
        for i in range(K_COUNT):
            doc_copy(i).start()

    top, total = row_partial([s_own, s_right])
    row_top[...] = jnp.broadcast_to(top, row_top.shape)
    row_sum[...] = jnp.broadcast_to(total, row_sum.shape)

    for i in range(K_COUNT):
        doc_copy(i).wait_recv()
        tile_into(s_far, q, k_far, i * K_CHUNK, 1, K_CHUNK)

    far_top, far_total = row_partial([s_far])
    near_top = row_top[:, 0:1]
    top = jnp.maximum(near_top, far_top)
    row_lse = top + jnp.log(
        row_sum[:, 0:1] * jnp.exp(near_top - top) + far_total * jnp.exp(far_top - top)
    )
    far_top, far_total = column_partial([s_far])
    part_move.wait_recv()
    near_top = part_in[0:1, :]
    top = jnp.maximum(near_top, far_top)
    far_lse = top + jnp.log(
        part_in[1:2, :] * jnp.exp(near_top - top) + far_total * jnp.exp(far_top - top)
    )
    back_out[0:1, :] = far_lse
    back_move = remote(back_out, back_in, stat_send.at[1], stat_recv.at[1], far_partner)
    back_move.start()
    weights = jnp.exp(s_far[...] - row_lse) + jnp.exp(s_far[...] - far_lse)
    g_far[...] = weights.astype(jnp.bfloat16)
    gt_far[...] = weights.T.astype(jnp.bfloat16)

    @pl.loop(0, P_COUNT)
    def _(i):
        rows = pl.ds(pl.multiple_of(i * P_CHUNK, P_CHUNK), P_CHUNK)
        share_out[rows, :] = dot(gt_far[rows, :], q[...]).astype(jnp.bfloat16)
        share_copy(i).start()

    row_out[...] = jnp.broadcast_to(row_lse, row_out.shape)
    row_move = remote(row_out, row_in, stat_send.at[2], stat_recv.at[2], core_partner)
    row_move.start()
    back_move.wait_recv()
    col_out[0:1, :] = back_in[0:1, :]
    col_move = remote(col_out, col_in, stat_send.at[3], stat_recv.at[3], core_partner)
    col_move.start()
    column_lse = back_in[0:1, :]

    row_lse = row_out[:, 0:1]
    pair = jnp.broadcast_to(pair_ref[...].astype(jnp.float32), (128, ROWS)).T[:, 0:1]
    places = lax.broadcasted_iota(jnp.int32, (ROWS, ROWS), 1)
    onehot = (pair.astype(jnp.int32) == places).astype(jnp.float32)
    own = s_own[...]
    weights = jnp.exp(own - row_lse) + jnp.exp(own - column_lse) - 2.0 * onehot
    g_own[...] = weights.astype(jnp.bfloat16)
    gt_own[...] = weights.T.astype(jnp.bfloat16)
    positive = onehot * own
    row_loss = row_lse - positive.sum(axis=1, keepdims=True)
    loss[0:1, :] = jnp.broadcast_to(row_loss, (ROWS, 128)).T[0:1, :]
    loss[1:2, :] = column_lse - positive.sum(axis=0, keepdims=True)

    row_move.wait_recv()
    col_move.wait_recv()
    right = s_right[...]
    g_right[...] = (jnp.exp(right - row_lse) + jnp.exp(right - col_in[0:1, :])).astype(jnp.bfloat16)
    left = s_left[...]
    weights = jnp.exp(left - row_in[:, 0:1]) + jnp.exp(left - column_lse)
    gt_left[...] = weights.T.astype(jnp.bfloat16)

    @pl.loop(0, D // WIDE)
    def _(i):
        at = pl.ds(pl.multiple_of(i * WIDE, WIDE), WIDE)
        total = dot(g_own[...], k[:, at]) + dot(g_right[...], k_core[:, at])
        total = total + dot(g_far[...], k_far[:, at])
        dq[:, at] = (logit_scale * total).astype(jnp.bfloat16)
        acc[:, at] = dot(gt_own[...], q[:, at]) + dot(gt_left[...], q_core[:, at])

    @pl.loop(0, P_COUNT)
    def _(i):
        share_copy(i).wait_recv()
        rows = pl.ds(pl.multiple_of(i * P_CHUNK, P_CHUNK), P_CHUNK)
        total = acc[rows, :] + share_in[rows, :].astype(jnp.float32)
        dk[rows, :] = (logit_scale * total).astype(jnp.bfloat16)

    for i in range(K_COUNT):
        doc_copy(i).wait_send()

    @pl.loop(0, P_COUNT)
    def _(i):
        share_copy(i).wait_send()

    for move in (k_move, q_move, part_move, back_move, row_move, col_move):
        move.wait_send()


def finish(dq_in, dk_in, loss_in, dq, dk, row_loss, column_loss, sem):
    first = pltpu.make_async_copy(dq_in, dq, sem.at[0])
    second = pltpu.make_async_copy(dk_in, dk, sem.at[1])
    first.start()
    second.start()
    row_loss[...] = loss_in[0, :]
    column_loss[...] = loss_in[1, :]
    first.wait()
    second.wait()


def shards(queries, documents, pair_index):
    vmem = pl.BlockSpec(memory_space=pltpu.VMEM)
    anywhere = pl.BlockSpec(memory_space=pl.ANY)
    block = lambda *shape, dtype=jnp.bfloat16: pltpu.VMEM(shape, dtype)
    f32 = jnp.float32
    big = jax.ShapeDtypeStruct((ROWS, D), jnp.bfloat16)
    dq, dk, loss = pl.pallas_call(
        exchange,
        out_shape=(big, big, jax.ShapeDtypeStruct((8, ROWS), f32)),
        in_specs=[anywhere, anywhere, vmem],
        out_specs=(vmem, vmem, vmem),
        scratch_shapes=[block(ROWS, D) for _ in range(7)]
        + [block(ROWS, D, dtype=f32)]
        + [block(ROWS, ROWS, dtype=f32) for _ in range(4)]
        + [block(ROWS, ROWS) for _ in range(6)]
        + [block(ROWS, 128, dtype=f32) for _ in range(4)]
        + [block(8, ROWS, dtype=f32) for _ in range(6)]
        + [
            pltpu.SemaphoreType.DMA((n,))
            for n in (2, K_COUNT, K_COUNT, 2, 2, 4, 4, P_COUNT, P_COUNT)
        ],
        compiler_params=pltpu.CompilerParams(
            collective_id=0, has_side_effects=True, vmem_limit_bytes=60 << 20
        ),
        cost_estimate=pl.CostEstimate(
            flops=20 * ROWS * ROWS * D, bytes_accessed=16 * ROWS * D, transcendentals=8 * ROWS * ROWS
        ),
    )(queries, documents, pair_index)
    vector = jax.ShapeDtypeStruct((ROWS,), f32)
    return pl.pallas_call(
        finish,
        out_shape=(big, big, vector, vector),
        in_specs=[vmem, vmem, vmem],
        out_specs=(anywhere, anywhere, vmem, vmem),
        scratch_shapes=[pltpu.SemaphoreType.DMA((2,))],
        compiler_params=pltpu.CompilerParams(vmem_limit_bytes=16 << 20),
    )(dq, dk, loss)


def solution(mesh):
    rows = P(("grp", "dev"), None)
    flat = P(("grp", "dev"))
    return jax.shard_map(
        shards,
        mesh=mesh,
        in_specs=(rows, rows, rows),
        out_specs=(rows, rows, flat, flat),
        check_vma=False,
    )
```

time: 218 us -> 201 us (0.922)
  Pallas kernels: 0 us -> 195 us
  waiting for transfers between devices: 152 us -> 0 us
  matrix products: 43.5 us -> 0 us
  starting transfers between devices: 17.7 us -> 0 us
  local copies, waits for them, and re-layouts: 0.02 us -> 5.09 us
  other arithmetic: 2.39 us -> 0 us
    pallas_call x0 -> x2, Pallas kernels: none -> 195 us  [the longest x1 191 us: shards(): pl.pallas_call(exchange, out_shape=(big, big, jax.ShapeDtypeStruct((8, RO...]
    ppermute x10 -> x0, waiting for transfers between devices: 152 us -> none  [swapped(): return lax.ppermute(block, axis, route)]
    dot_general x9 -> x0, matrix products: 43.5 us -> none  [the longest x3 16.4 us: apply_left(): return jnp.dot(weights, right_rows, preferred_element_type=jnp.float32)]
    ppermute x10 -> x0, starting transfers between devices: 17.7 us -> none  [swapped(): return lax.ppermute(block, axis, route)]
    unnamed x8 -> x6, local copies, waits for them, and re-layouts: 0.02 us -> 5.09 us
  transfers between devices with their start and end apart: 10 -> 0, of which waited for: 4 -> 0; matrix products, arithmetic and copies ran while one was open for 17% -> 0% of each run, Pallas kernels for 0% -> 0%
where the time goes in v1:
time: 201 us
  Pallas kernels  195 us (97%)
  local copies, waits for them, and re-layouts  5.09 us (3%)
    pallas_call x1, Pallas kernels, shards(): pl.pallas_call(exchange, out_shape=(big, big, jax.ShapeDtypeStruct((8, RO...  191 us
    unnamed x6, local copies, waits for them, and re-layouts  5.09 us

profile of v1, /device:TPU:1, one launch (start us, length us, event | category | flops | bytes accessed | tf_op | source)
XLA Modules:
  0.0 200.7 jit_solution(4657749637482269437)
XLA Ops:
  0.6 190.9 %shard_map.66 = (bf16[512,4096]{1,0:T(8,128)(2,1)}, bf16[512,4096]{1,0:T(8,128)(2,1)}, f32[8,512]{1,0:T(8,128)}) custom-call(bf16[512,4096]{1,0:T(8,128)(2,1)} %q_hbm.1, bf16[512,4096]{1,0:T(8,128)(2,1)} %k_hbm.1, s32[1,512]{1,0:T(1,128)} %pair_ref.1), custom_call_target="tpu_custom_call" | custom-call | flops 21474836480 | bytes 33554432 | tf_op jit(solution)/shard_map/pallas_call | solution.py:232
  191.6 0.0 copy-start
  191.6 2.2 %copy-done = bf16[512,4096]{1,0:T(8,128)(2,1)S(1)} copy-done((bf16[512,4096]{1,0:T(8,128)(2,1)S(1)}, bf16[512,4096]{1,0:T(8,128)(2,1)}, u32[]{:S(2)}) %copy-start) | copy-done | bytes 4194328
  193.8 0.0 copy-start.1
  193.8 2.2 %copy-done.1 = bf16[512,4096]{1,0:T(8,128)(2,1)S(1)} copy-done((bf16[512,4096]{1,0:T(8,128)(2,1)S(1)}, bf16[512,4096]{1,0:T(8,128)(2,1)}, u32[]{:S(2)}) %copy-start.1) | copy-done | bytes 4194328
  196.0 0.0 copy-start.2
  196.0 0.7 copy-done.2
  196.7 4.0 %shard_map.67 = (bf16[512,4096]{1,0:T(8,128)(2,1)}, bf16[512,4096]{1,0:T(8,128)(2,1)}, f32[512]{0:T(512)}, f32[512]{0:T(512)}) custom-call(bf16[512,4096]{1,0:T(8,128)(2,1)S(1)} %copy-done, bf16[512,4096]{1,0:T(8,128)(2,1)S(1)} %copy-done.1, f32[8,512]{1,0:T(8,128)S(1)} %copy-done.2), custom_call_target="tpu_custom_call" | custom-call | tf_op jit(solution)/shard_map/pallas_call | solution.py:255
Async XLA Ops:
  191.6 2.2 %copy-start = (bf16[512,4096]{1,0:T(8,128)(2,1)S(1)}, bf16[512,4096]{1,0:T(8,128)(2,1)}, u32[]{:S(2)}) copy-start(bf16[512,4096]{1,0:T(8,128)(2,1)} %get-tuple-element.7.dq_in) | copy-start | bytes 12582916
  193.8 2.2 %copy-start.1 = (bf16[512,4096]{1,0:T(8,128)(2,1)S(1)}, bf16[512,4096]{1,0:T(8,128)(2,1)}, u32[]{:S(2)}) copy-start(bf16[512,4096]{1,0:T(8,128)(2,1)} %get-tuple-element.8.dk_in) | copy-start | bytes 12582916
  196.0 0.7 copy-start.2

commit v2 on v1

--- a/solution.py
+++ b/solution.py
@@ -11,9 +11,11 @@
 D = 4096
 K_CHUNK = 128
 K_COUNT = ROWS // K_CHUNK
-P_CHUNK = 64
-P_COUNT = ROWS // P_CHUNK
-WIDE = 512
+P_CHUNK = 128
+LAST = 128
+HEAD = ROWS - LAST
+P_COUNT = HEAD // P_CHUNK
+WIDE = 1024
 
 
 def tile_into(out, left, right, first, count, step):
@@ -53,14 +55,14 @@
 
 
 def exchange(
-    q_hbm, k_hbm, pair_ref, dq, dk, loss,
-    q, k, q_core, k_core, k_far, share_out, share_in, acc,
+    q_hbm, k_hbm, pair_ref, dq_hbm, dk_hbm, share_hbm, acc_hbm, loss,
+    q, k, q_core, k_core, k_far, share_out, dq, share_in, dk, acc,
     s_own, s_right, s_left, s_far,
     g_own, g_right, g_far, gt_own, gt_left, gt_far,
     row_top, row_sum, row_out, row_in, part_out, part_in,
     back_out, back_in, col_out, col_in,
     local_sem, doc_send, doc_recv, core_send, core_recv, stat_send, stat_recv,
-    share_send, share_recv,
+    share_send, share_recv, out_sem, dk_sem,
 ):
     g = lax.axis_index("grp")
     d = lax.axis_index("dev")
@@ -109,6 +111,11 @@
     k_move.wait_recv()
     tile_into(s_right, q, k_core, 0, 2, 256)
     q_move.wait_recv()
+    @pl.when(core == 1)
+    def _():
+        for i in range(K_COUNT):
+            doc_copy(i).start()
+
     tile_into(s_left, q_core, k, 0, 2, 256)
 
     top, total = column_partial([s_own, s_left])
@@ -116,11 +123,6 @@
     part_out[1:2, :] = total
     part_move = remote(part_out, part_in, stat_send.at[0], stat_recv.at[0], far_partner)
     part_move.start()
-
-    @pl.when(core == 1)
-    def _():
-        for i in range(K_COUNT):
-            doc_copy(i).start()
 
     top, total = row_partial([s_own, s_right])
     row_top[...] = jnp.broadcast_to(top, row_top.shape)
@@ -156,6 +158,11 @@
         share_out[rows, :] = dot(gt_far[rows, :], q[...]).astype(jnp.bfloat16)
         share_copy(i).start()
 
+    tail = pl.ds(HEAD, LAST)
+    share_out[tail, :] = dot(gt_far[tail, :], q[...]).astype(jnp.bfloat16)
+    share_store = pltpu.make_async_copy(share_out.at[tail], share_hbm, out_sem.at[0])
+    share_store.start()
+
     row_out[...] = jnp.broadcast_to(row_lse, row_out.shape)
     row_move = remote(row_out, row_in, stat_send.at[2], stat_recv.at[2], core_partner)
     row_move.start()
@@ -194,12 +201,22 @@
         dq[:, at] = (logit_scale * total).astype(jnp.bfloat16)
         acc[:, at] = dot(gt_own[...], q[:, at]) + dot(gt_left[...], q_core[:, at])
 
+    dq_store = pltpu.make_async_copy(dq, dq_hbm, out_sem.at[1])
+    dq_store.start()
+    acc_store = pltpu.make_async_copy(acc.at[tail], acc_hbm, out_sem.at[2])
+    acc_store.start()
+
+    def dk_store(i):
+        rows = pl.ds(pl.multiple_of(i * P_CHUNK, P_CHUNK), P_CHUNK)
+        return pltpu.make_async_copy(dk.at[rows], dk_hbm.at[rows], dk_sem.at[i])
+
     @pl.loop(0, P_COUNT)
     def _(i):
         share_copy(i).wait_recv()
         rows = pl.ds(pl.multiple_of(i * P_CHUNK, P_CHUNK), P_CHUNK)
         total = acc[rows, :] + share_in[rows, :].astype(jnp.float32)
         dk[rows, :] = (logit_scale * total).astype(jnp.bfloat16)
+        dk_store(i).start()
 
     for i in range(K_COUNT):
         doc_copy(i).wait_send()
@@ -207,14 +224,17 @@
     @pl.loop(0, P_COUNT)
     def _(i):
         share_copy(i).wait_send()
-
+        dk_store(i).wait()
+
+    for store in (share_store, dq_store, acc_store):
+        store.wait()
     for move in (k_move, q_move, part_move, back_move, row_move, col_move):
         move.wait_send()
 
 
-def finish(dq_in, dk_in, loss_in, dq, dk, row_loss, column_loss, sem):
+def settle(dq_in, dk_in, loss_in, dq, dk, row_loss, column_loss, sem):
     first = pltpu.make_async_copy(dq_in, dq, sem.at[0])
-    second = pltpu.make_async_copy(dk_in, dk, sem.at[1])
+    second = pltpu.make_async_copy(dk_in, dk.at[pl.ds(0, HEAD)], sem.at[1])
     first.start()
     second.start()
     row_loss[...] = loss_in[0, :]
@@ -223,18 +243,28 @@
     second.wait()
 
 
+def finish(acc, share, dk_in, dk, out, sem):
+    total = acc[...] + share[...].astype(jnp.float32)
+    out[...] = (logit_scale * total).astype(jnp.bfloat16)
+    store = pltpu.make_async_copy(out, dk.at[pl.ds(HEAD, LAST)], sem)
+    store.start()
+    store.wait()
+
+
 def shards(queries, documents, pair_index):
     vmem = pl.BlockSpec(memory_space=pltpu.VMEM)
     anywhere = pl.BlockSpec(memory_space=pl.ANY)
-    block = lambda *shape, dtype=jnp.bfloat16: pltpu.VMEM(shape, dtype)
-    f32 = jnp.float32
-    big = jax.ShapeDtypeStruct((ROWS, D), jnp.bfloat16)
-    dq, dk, loss = pl.pallas_call(
+    f32, bf16 = jnp.float32, jnp.bfloat16
+    block = lambda *shape, dtype=bf16: pltpu.VMEM(shape, dtype)
+    out = jax.ShapeDtypeStruct
+    big = out((ROWS, D), bf16)
+    dq, dk_head, share_tail, acc_tail, loss = pl.pallas_call(
         exchange,
-        out_shape=(big, big, jax.ShapeDtypeStruct((8, ROWS), f32)),
+        out_shape=(big, out((HEAD, D), bf16), out((LAST, D), bf16), out((LAST, D), f32), out((8, ROWS), f32)),
         in_specs=[anywhere, anywhere, vmem],
-        out_specs=(vmem, vmem, vmem),
+        out_specs=(anywhere, anywhere, anywhere, anywhere, vmem),
         scratch_shapes=[block(ROWS, D) for _ in range(7)]
+        + [block(HEAD, D) for _ in range(2)]
         + [block(ROWS, D, dtype=f32)]
         + [block(ROWS, ROWS, dtype=f32) for _ in range(4)]
         + [block(ROWS, ROWS) for _ in range(6)]
@@ -242,7 +272,7 @@
         + [block(8, ROWS, dtype=f32) for _ in range(6)]
         + [
             pltpu.SemaphoreType.DMA((n,))
-            for n in (2, K_COUNT, K_COUNT, 2, 2, 4, 4, P_COUNT, P_COUNT)
+            for n in (2, K_COUNT, K_COUNT, 2, 2, 4, 4, P_COUNT, P_COUNT, 3, P_COUNT)
         ],
         compiler_params=pltpu.CompilerParams(
             collective_id=0, has_side_effects=True, vmem_limit_bytes=60 << 20
@@ -251,15 +281,30 @@
             flops=20 * ROWS * ROWS * D, bytes_accessed=16 * ROWS * D, transcendentals=8 * ROWS * ROWS
         ),
     )(queries, documents, pair_index)
-    vector = jax.ShapeDtypeStruct((ROWS,), f32)
-    return pl.pallas_call(
-        finish,
+    grp_count, dev_count = lax.axis_size("grp"), lax.axis_size("dev")
+    route = [(i, i ^ (dev_count // 2)) for i in range(grp_count * dev_count)]
+    share = lax.ppermute(share_tail, ("grp", "dev"), route)
+    vector = out((ROWS,), f32)
+    dq, dk, row_loss, column_loss = pl.pallas_call(
+        settle,
         out_shape=(big, big, vector, vector),
-        in_specs=[vmem, vmem, vmem],
+        in_specs=[anywhere, anywhere, vmem],
         out_specs=(anywhere, anywhere, vmem, vmem),
         scratch_shapes=[pltpu.SemaphoreType.DMA((2,))],
         compiler_params=pltpu.CompilerParams(vmem_limit_bytes=16 << 20),
-    )(dq, dk, loss)
+        cost_estimate=pl.CostEstimate(flops=0, bytes_accessed=8 * ROWS * D, transcendentals=0),
+    )(dq, dk_head, loss)
+    dk = pl.pallas_call(
+        finish,
+        out_shape=big,
+        in_specs=[vmem, vmem, anywhere],
+        out_specs=anywhere,
+        input_output_aliases={2: 0},
+        scratch_shapes=[block(LAST, D), pltpu.SemaphoreType.DMA],
+        compiler_params=pltpu.CompilerParams(vmem_limit_bytes=16 << 20),
+        cost_estimate=pl.CostEstimate(flops=2 * LAST * D, bytes_accessed=8 * LAST * D, transcendentals=0),
+    )(acc_tail, share, dk)
+    return dq, dk, row_loss, column_loss
 
 
 def solution(mesh):

time: 201 us -> 190 us (0.945)
  Pallas kernels: 195 us -> 174 us
  waiting for transfers between devices: 0 us -> 6.89 us
  starting transfers between devices: 0 us -> 2.82 us
    pallas_call x2 -> x3, Pallas kernels: 195 us -> 174 us  [the longest x1 169 us: shards(): pl.pallas_call(exchange, out_shape=(big, out((HEAD, D), bf16), out((LAST,...]
    ppermute x0 -> x1, waiting for transfers between devices: none -> 6.89 us  [shards(): share = lax.ppermute(share_tail, ('grp', 'dev'), route)]
    ppermute x0 -> x1, starting transfers between devices: none -> 2.82 us  [shards(): share = lax.ppermute(share_tail, ('grp', 'dev'), route)]
    unnamed x6 -> x8, local copies, waits for them, and re-layouts: 5.09 us -> 4.8 us
  transfers between devices with their start and end apart: 0 -> 1, of which waited for: 0 -> 1; matrix products, arithmetic and copies ran while one was open for 0% -> 0% of each run, Pallas kernels for 0% -> 2%
where the time goes in v2:
time: 190 us; the launch traced here: 189 us
  Pallas kernels  174 us (92%)
  waiting for transfers between devices  6.89 us (4%)
  local copies, waits for them, and re-layouts  4.8 us (3%)
  starting transfers between devices  2.82 us (1%)
    pallas_call x1, Pallas kernels, shards(): pl.pallas_call(exchange, out_shape=(big, out((HEAD, D), bf16), out((LAST,...  169 us
    ppermute x1, waiting for transfers between devices, shards(): share = lax.ppermute(share_tail, ('grp', 'dev'), route)  6.89 us
    unnamed x8, local copies, waits for them, and re-layouts  4.8 us
  transfers between devices with their start and end apart: 1, of which 1 were waited for; matrix products, arithmetic and copies ran while one was open for 0% of the time, Pallas kernels for 2%

profile of v2, /device:TPU:1, one launch (start us, length us, event | category | flops | bytes accessed | tf_op | source)
XLA Modules:
  0.0 189.2 jit_solution(2137703879167302921)
XLA Ops:
  0.6 169.0 %shard_map.66 = (bf16[512,4096]{1,0:T(8,128)(2,1)}, bf16[384,4096]{1,0:T(8,128)(2,1)}, bf16[128,4096]{1,0:T(8,128)(2,1)}, f32[128,4096]{1,0:T(8,128)}, f32[8,512]{1,0:T(8,128)}) custom-call(bf16[512,4096]{1,0:T(8,128)(2,1)} %q_hbm.1, bf16[512,4096]{1,0:T(8,128)(2,1)} %k_hbm.1, s32[1,512]{1,0:T(1,128)} %pair_ref.1), custom_call_target="tpu_custom_call" | custom-call | flops 21474836480 | bytes 33554432 | tf_op jit(solution)/shard_map/pallas_call | solution.py:261
  169.7 2.8 %collective-permute-start = (bf16[128,4096]{1,0:T(8,128)(2,1)}, bf16[128,4096]{1,0:T(8,128)(2,1)S(1)}, u32[]{:S(2)}, u32[]{:S(2)}) collective-permute-start(bf16[128,4096]{1,0:T(8,128)(2,1)} %get-tuple-element.18), channel_id=1, source_target_pairs={{0,16},{1,17},{2,18},{3,19},{4,20},{5,21},{6,22},{7,23},{8,24},{9,... | collective-permute-start | bytes 3145736 | tf_op jit(solution)/shard_map/ppermute | solution.py:286
  172.5 0.0 copy-start
  172.5 2.2 %copy-done = bf16[512,4096]{1,0:T(8,128)(2,1)S(1)} copy-done((bf16[512,4096]{1,0:T(8,128)(2,1)S(1)}, bf16[512,4096]{1,0:T(8,128)(2,1)}, u32[]{:S(2)}) %copy-start) | copy-done | bytes 4194328
  174.7 0.0 copy-start.1
  174.7 1.9 copy-done.1
  176.6 0.0 copy-start.3
  176.6 0.7 copy-done.3
  177.3 0.0 copy-start.2
  177.3 3.7 %shard_map.67 = (bf16[512,4096]{1,0:T(8,128)(2,1)}, bf16[512,4096]{1,0:T(8,128)(2,1)}, f32[512]{0:T(512)}, f32[512]{0:T(512)}) custom-call(bf16[512,4096]{1,0:T(8,128)(2,1)S(1)} %copy-done, bf16[384,4096]{1,0:T(8,128)(2,1)S(1)} %copy-done.1, f32[8,512]{1,0:T(8,128)S(1)} %copy-done.3), custom_call_target="tpu_custom_call" | custom-call | bytes 16777216 | tf_op jit(solution)/shard_map/pallas_call | solution.py:288
  181.0 6.9 %collective-permute-done.share = bf16[128,4096]{1,0:T(8,128)(2,1)S(1)} collective-permute-done((bf16[128,4096]{1,0:T(8,128)(2,1)}, bf16[128,4096]{1,0:T(8,128)(2,1)S(1)}, u32[]{:S(2)}, u32[]{:S(2)}) %collective-permute-start) | collective-permute-done | bytes 1048608 | tf_op jit(solution)/shard_map/ppermute | solution.py:286
  187.9 0.0 copy-done.2
  187.9 1.2 shard_map.68
Async XLA Ops:
  169.7 18.2 %collective-permute-start = (bf16[128,4096]{1,0:T(8,128)(2,1)}, bf16[128,4096]{1,0:T(8,128)(2,1)S(1)}, u32[]{:S(2)}, u32[]{:S(2)}) collective-permute-start(bf16[128,4096]{1,0:T(8,128)(2,1)} %get-tuple-element.18), channel_id=1, source_target_pairs={{0,16},{1,17},{2,18},{3,19},{4,20},{5,21},{6,22},{7,23},{8,24},{9,... | collective-permute-start | bytes 3145736 | tf_op jit(solution)/shard_map/ppermute | solution.py:286
  172.5 2.2 %copy-start = (bf16[512,4096]{1,0:T(8,128)(2,1)S(1)}, bf16[512,4096]{1,0:T(8,128)(2,1)}, u32[]{:S(2)}) copy-start(bf16[512,4096]{1,0:T(8,128)(2,1)} %get-tuple-element.13.dq_in) | copy-start | bytes 12582916
  174.7 1.9 copy-start.1
  176.6 0.7 copy-start.3
  177.3 10.6 %copy-start.2 = (f32[128,4096]{1,0:T(8,128)S(1)}, f32[128,4096]{1,0:T(8,128)}, u32[]{:S(2)}) copy-start(f32[128,4096]{1,0:T(8,128)} %get-tuple-element.17.acc) | copy-start | bytes 6291460

commit v3 on v2

--- a/solution.py
+++ b/solution.py
@@ -9,13 +9,14 @@
 MESH = pl.DeviceIdType.MESH
 ROWS = 512
 D = 4096
-K_CHUNK = 128
+K_CHUNK = 256
 K_COUNT = ROWS // K_CHUNK
 P_CHUNK = 128
 LAST = 128
 HEAD = ROWS - LAST
 P_COUNT = HEAD // P_CHUNK
 WIDE = 1024
+SLAB = 64
 
 
 def tile_into(out, left, right, first, count, step):
@@ -55,12 +56,12 @@
 
 
 def exchange(
-    q_hbm, k_hbm, pair_ref, dq_hbm, dk_hbm, share_hbm, acc_hbm, loss,
+    q_hbm, k_hbm, pair_hbm, dq_hbm, dk_hbm, share_hbm, acc_hbm, loss_hbm,
     q, k, q_core, k_core, k_far, share_out, dq, share_in, dk, acc,
     s_own, s_right, s_left, s_far,
     g_own, g_right, g_far, gt_own, gt_left, gt_far,
     row_top, row_sum, row_out, row_in, part_out, part_in,
-    back_out, back_in, col_out, col_in,
+    back_out, back_in, col_out, col_in, loss, pair_ref,
     local_sem, doc_send, doc_recv, core_send, core_recv, stat_send, stat_recv,
     share_send, share_recv, out_sem, dk_sem,
 ):
@@ -101,12 +102,15 @@
     q_move = remote(q_hbm, q_core, core_send.at[1], core_recv.at[1], core_partner)
     q_load = pltpu.make_async_copy(q_hbm, q, local_sem.at[0])
     k_load = pltpu.make_async_copy(k_hbm, k, local_sem.at[1])
+    pair_load = pltpu.make_async_copy(pair_hbm, pair_ref, local_sem.at[2])
     q_load.start()
     k_load.start()
+    pair_load.start()
     k_move.start()
     q_move.start()
     q_load.wait()
     k_load.wait()
+    pair_load.wait()
     tile_into(s_own, q, k, 0, 2, 256)
     k_move.wait_recv()
     tile_into(s_right, q, k_core, 0, 2, 256)
@@ -185,6 +189,9 @@
     loss[0:1, :] = jnp.broadcast_to(row_loss, (ROWS, 128)).T[0:1, :]
     loss[1:2, :] = column_lse - positive.sum(axis=0, keepdims=True)
 
+    loss_store = pltpu.make_async_copy(loss, loss_hbm, out_sem.at[3])
+    loss_store.start()
+
     row_move.wait_recv()
     col_move.wait_recv()
     right = s_right[...]
@@ -226,29 +233,47 @@
         share_copy(i).wait_send()
         dk_store(i).wait()
 
-    for store in (share_store, dq_store, acc_store):
+    for store in (share_store, dq_store, acc_store, loss_store):
         store.wait()
     for move in (k_move, q_move, part_move, back_move, row_move, col_move):
         move.wait_send()
 
 
-def settle(dq_in, dk_in, loss_in, dq, dk, row_loss, column_loss, sem):
-    first = pltpu.make_async_copy(dq_in, dq, sem.at[0])
-    second = pltpu.make_async_copy(dk_in, dk.at[pl.ds(0, HEAD)], sem.at[1])
-    first.start()
-    second.start()
-    row_loss[...] = loss_in[0, :]
-    column_loss[...] = loss_in[1, :]
-    first.wait()
-    second.wait()
+def settle(dq_in, dk_in, loss_in, dq, dk, row_loss, column_loss, held, loss, load_sem, store_sem, sem):
+    parts = [(dq_in, dq, r) for r in range(0, ROWS, SLAB)] + [(dk_in, dk, r) for r in range(0, HEAD, SLAB)]
+
+    def load(i):
+        src, _, r = parts[i]
+        return pltpu.make_async_copy(src.at[pl.ds(r, SLAB)], held.at[i], load_sem.at[i])
+
+    def store(i):
+        _, dst, r = parts[i]
+        return pltpu.make_async_copy(held.at[i], dst.at[pl.ds(r, SLAB)], store_sem.at[i])
+
+    loss_load = pltpu.make_async_copy(loss_in, loss, sem)
+    loss_load.start()
+    for i in range(len(parts)):
+        load(i).start()
+    loss_load.wait()
+    row_loss[...] = loss[0, :]
+    column_loss[...] = loss[1, :]
+    for i in range(len(parts)):
+        load(i).wait()
+        store(i).start()
+    for i in range(len(parts)):
+        store(i).wait()
 
 
 def finish(acc, share, dk_in, dk, out, sem):
-    total = acc[...] + share[...].astype(jnp.float32)
-    out[...] = (logit_scale * total).astype(jnp.bfloat16)
-    store = pltpu.make_async_copy(out, dk.at[pl.ds(HEAD, LAST)], sem)
-    store.start()
-    store.wait()
+    stores = []
+    for r in range(0, LAST, LAST // 4):
+        part = pl.ds(r, LAST // 4)
+        total = acc[part, :] + share[part, :].astype(jnp.float32)
+        out[part, :] = (logit_scale * total).astype(jnp.bfloat16)
+        stores.append(pltpu.make_async_copy(out.at[part], dk.at[pl.ds(HEAD + r, LAST // 4)], sem.at[len(stores)]))
+        stores[-1].start()
+    for store in stores:
+        store.wait()
 
 
 def shards(queries, documents, pair_index):
@@ -261,18 +286,19 @@
     dq, dk_head, share_tail, acc_tail, loss = pl.pallas_call(
         exchange,
         out_shape=(big, out((HEAD, D), bf16), out((LAST, D), bf16), out((LAST, D), f32), out((8, ROWS), f32)),
-        in_specs=[anywhere, anywhere, vmem],
-        out_specs=(anywhere, anywhere, anywhere, anywhere, vmem),
+        in_specs=[anywhere, anywhere, anywhere],
+        out_specs=(anywhere, anywhere, anywhere, anywhere, anywhere),
         scratch_shapes=[block(ROWS, D) for _ in range(7)]
         + [block(HEAD, D) for _ in range(2)]
         + [block(ROWS, D, dtype=f32)]
         + [block(ROWS, ROWS, dtype=f32) for _ in range(4)]
         + [block(ROWS, ROWS) for _ in range(6)]
         + [block(ROWS, 128, dtype=f32) for _ in range(4)]
-        + [block(8, ROWS, dtype=f32) for _ in range(6)]
+        + [block(8, ROWS, dtype=f32) for _ in range(7)]
+        + [block(1, ROWS, dtype=jnp.int32)]
         + [
             pltpu.SemaphoreType.DMA((n,))
-            for n in (2, K_COUNT, K_COUNT, 2, 2, 4, 4, P_COUNT, P_COUNT, 3, P_COUNT)
+            for n in (3, K_COUNT, K_COUNT, 2, 2, 4, 4, P_COUNT, P_COUNT, 4, P_COUNT)
         ],
         compiler_params=pltpu.CompilerParams(
             collective_id=0, has_side_effects=True, vmem_limit_bytes=60 << 20
@@ -288,10 +314,16 @@
     dq, dk, row_loss, column_loss = pl.pallas_call(
         settle,
         out_shape=(big, big, vector, vector),
-        in_specs=[anywhere, anywhere, vmem],
+        in_specs=[anywhere, anywhere, anywhere],
         out_specs=(anywhere, anywhere, vmem, vmem),
-        scratch_shapes=[pltpu.SemaphoreType.DMA((2,))],
-        compiler_params=pltpu.CompilerParams(vmem_limit_bytes=16 << 20),
+        scratch_shapes=[
+            block((ROWS + HEAD) // SLAB, SLAB, D),
+            block(8, ROWS, dtype=f32),
+            pltpu.SemaphoreType.DMA(((ROWS + HEAD) // SLAB,)),
+            pltpu.SemaphoreType.DMA(((ROWS + HEAD) // SLAB,)),
+            pltpu.SemaphoreType.DMA,
+        ],
+        compiler_params=pltpu.CompilerParams(vmem_limit_bytes=60 << 20),
         cost_estimate=pl.CostEstimate(flops=0, bytes_accessed=8 * ROWS * D, transcendentals=0),
     )(dq, dk_head, loss)
     dk = pl.pallas_call(
@@ -300,7 +332,7 @@
         in_specs=[vmem, vmem, anywhere],
         out_specs=anywhere,
         input_output_aliases={2: 0},
-        scratch_shapes=[block(LAST, D), pltpu.SemaphoreType.DMA],
+        scratch_shapes=[block(LAST, D), pltpu.SemaphoreType.DMA((4,))],
         compiler_params=pltpu.CompilerParams(vmem_limit_bytes=16 << 20),
         cost_estimate=pl.CostEstimate(flops=2 * LAST * D, bytes_accessed=8 * LAST * D, transcendentals=0),
     )(acc_tail, share, dk)

time: 190 us -> 188 us (0.989)
  local copies, waits for them, and re-layouts: 4.8 us -> 0.01 us
  Pallas kernels: 174 us -> 176 us
  waiting for transfers between devices: 6.89 us -> 8.83 us
    unnamed x8 -> x2, local copies, waits for them, and re-layouts: 4.8 us -> 0.01 us
    pallas_call x1, Pallas kernels: 3.69 us -> 6.54 us  [shards(): pl.pallas_call(settle, out_shape=(big, big, vector, vector), in_specs=[an...]
    ppermute x1, waiting for transfers between devices: 6.89 us -> 8.83 us  [shards(): share = lax.ppermute(share_tail, ('grp', 'dev'), route)]
  transfers between devices with their start and end apart: 1 -> 1, of which waited for: 1 -> 1; matrix products, arithmetic and copies ran while one was open for 0% -> 0% of each run, Pallas kernels for 2% -> 3%
where the time goes in v3:
time: 188 us
  Pallas kernels  176 us (94%)
  waiting for transfers between devices  8.83 us (5%)
  starting transfers between devices  2.83 us (2%)
    pallas_call x1, Pallas kernels, shards(): pl.pallas_call(exchange, out_shape=(big, out((HEAD, D), bf16), out((LAST,...  168 us
    ppermute x1, waiting for transfers between devices, shards(): share = lax.ppermute(share_tail, ('grp', 'dev'), route)  8.83 us
    pallas_call x1, Pallas kernels, shards(): pl.pallas_call(settle, out_shape=(big, big, vector, vector), in_specs=[an...  6.54 us
  transfers between devices with their start and end apart: 1, of which 1 were waited for; matrix products, arithmetic and copies ran while one was open for 0% of the time, Pallas kernels for 3%

profile of v3, /device:TPU:1, one launch (start us, length us, event | category | flops | bytes accessed | tf_op | source)
XLA Modules:
  0.0 188.3 jit_solution(8009945748511352933)
XLA Ops:
  0.6 168.3 %shard_map.66 = (bf16[512,4096]{1,0:T(8,128)(2,1)}, bf16[384,4096]{1,0:T(8,128)(2,1)}, bf16[128,4096]{1,0:T(8,128)(2,1)}, f32[128,4096]{1,0:T(8,128)}, f32[8,512]{1,0:T(8,128)}) custom-call(bf16[512,4096]{1,0:T(8,128)(2,1)} %q_hbm.1, bf16[512,4096]{1,0:T(8,128)(2,1)} %k_hbm.1, s32[1,512]{1,0:T(1,128)} %pair_hbm.1), custom_call_target="tpu_custom_call" | custom-call | flops 21474836480 | bytes 33554432 | tf_op jit(solution)/shard_map/pallas_call | solution.py:286
  169.0 0.0 copy-start
  169.0 2.8 %collective-permute-start = (bf16[128,4096]{1,0:T(8,128)(2,1)}, bf16[128,4096]{1,0:T(8,128)(2,1)S(1)}, u32[]{:S(2)}, u32[]{:S(2)}) collective-permute-start(bf16[128,4096]{1,0:T(8,128)(2,1)} %get-tuple-element.18), channel_id=1, source_target_pairs={{0,16},{1,17},{2,18},{3,19},{4,20},{5,21},{6,22},{7,23},{8,24},{9,... | collective-permute-start | bytes 3145736 | tf_op jit(solution)/shard_map/ppermute | solution.py:312
  171.8 6.5 %shard_map.67 = (bf16[512,4096]{1,0:T(8,128)(2,1)}, bf16[512,4096]{1,0:T(8,128)(2,1)}, f32[512]{0:T(512)}, f32[512]{0:T(512)}) custom-call(bf16[512,4096]{1,0:T(8,128)(2,1)} %get-tuple-element.13.dq_in, bf16[384,4096]{1,0:T(8,128)(2,1)} %get-tuple-element.14.dk_in, f32[8,512]{1,0:T(8,128)} %get-tuple-element.15.loss_in), custom_call_target="tpu_custom_call" | custom-call | bytes 16777216 | tf_op jit(solution)/shard_map/pallas_call | solution.py:314
  178.4 8.8 %collective-permute-done.share = bf16[128,4096]{1,0:T(8,128)(2,1)S(1)} collective-permute-done((bf16[128,4096]{1,0:T(8,128)(2,1)}, bf16[128,4096]{1,0:T(8,128)(2,1)S(1)}, u32[]{:S(2)}, u32[]{:S(2)}) %collective-permute-start) | collective-permute-done | bytes 1048608 | tf_op jit(solution)/shard_map/ppermute | solution.py:312
  187.2 0.0 copy-done
  187.2 1.1 shard_map.68
Async XLA Ops:
  169.0 18.2 %copy-start = (f32[128,4096]{1,0:T(8,128)S(1)}, f32[128,4096]{1,0:T(8,128)}, u32[]{:S(2)}) copy-start(f32[128,4096]{1,0:T(8,128)} %get-tuple-element.17.acc) | copy-start | bytes 6291460
  169.0 18.2 %collective-permute-start = (bf16[128,4096]{1,0:T(8,128)(2,1)}, bf16[128,4096]{1,0:T(8,128)(2,1)S(1)}, u32[]{:S(2)}, u32[]{:S(2)}) collective-permute-start(bf16[128,4096]{1,0:T(8,128)(2,1)} %get-tuple-element.18), channel_id=1, source_target_pairs={{0,16},{1,17},{2,18},{3,19},{4,20},{5,21},{6,22},{7,23},{8,24},{9,... | collective-permute-start | bytes 3145736 | tf_op jit(solution)/shard_map/ppermute | solution.py:312

commit v4 on v3

--- a/solution.py
+++ b/solution.py
@@ -10,12 +10,13 @@
 ROWS = 512
 D = 4096
 K_CHUNK = 256
-K_COUNT = ROWS // K_CHUNK
+K_COUNT = D // K_CHUNK
+AHEAD = 3
 P_CHUNK = 128
 LAST = 128
 HEAD = ROWS - LAST
 P_COUNT = HEAD // P_CHUNK
-WIDE = 1024
+WIDE = 256
 SLAB = 64
 
 
@@ -63,7 +64,7 @@
     row_top, row_sum, row_out, row_in, part_out, part_in,
     back_out, back_in, col_out, col_in, loss, pair_ref,
     local_sem, doc_send, doc_recv, core_send, core_recv, stat_send, stat_recv,
-    share_send, share_recv, out_sem, dk_sem,
+    share_send, share_recv, out_sem, dk_sem, go_sem,
 ):
     g = lax.axis_index("grp")
     d = lax.axis_index("dev")
@@ -84,8 +85,10 @@
         )
 
     def doc_copy(i):
-        rows = pl.ds(i * K_CHUNK, K_CHUNK)
-        return remote(k_hbm.at[rows], k_far.at[rows], doc_send.at[i], doc_recv.at[i], far_partner)
+        part = pl.ds(pl.multiple_of(i * K_CHUNK, K_CHUNK), K_CHUNK)
+        return remote(
+            k_hbm.at[:, part], k_far.at[:, part], doc_send.at[i], doc_recv.at[i], far_partner
+        )
 
     def share_copy(i):
         rows = pl.ds(pl.multiple_of(i * P_CHUNK, P_CHUNK), P_CHUNK)
@@ -106,20 +109,33 @@
     q_load.start()
     k_load.start()
     pair_load.start()
-    k_move.start()
-    q_move.start()
+
+    @pl.when(core == 1)
+    def _():
+        k_move.start()
+        q_move.start()
+
     q_load.wait()
     k_load.wait()
     pair_load.wait()
     tile_into(s_own, q, k, 0, 2, 256)
+
+    @pl.when(core == 0)
+    def _():
+        doc_copy(AHEAD).wait_send()
+        pl.semaphore_signal(go_sem, inc=1, device_id=core_partner, device_id_type=MESH)
+        k_move.start()
+        q_move.start()
+
+    @pl.when(core == 1)
+    def _():
+        pl.semaphore_wait(go_sem, 1)
+        for i in range(K_COUNT):
+            doc_copy(i).start()
+
     k_move.wait_recv()
     tile_into(s_right, q, k_core, 0, 2, 256)
     q_move.wait_recv()
-    @pl.when(core == 1)
-    def _():
-        for i in range(K_COUNT):
-            doc_copy(i).start()
-
     tile_into(s_left, q_core, k, 0, 2, 256)
 
     top, total = column_partial([s_own, s_left])
@@ -132,9 +148,15 @@
     row_top[...] = jnp.broadcast_to(top, row_top.shape)
     row_sum[...] = jnp.broadcast_to(total, row_sum.shape)
 
-    for i in range(K_COUNT):
+    s_far[...] = jnp.zeros_like(s_far)
+
+    @pl.loop(0, K_COUNT)
+    def _(i):
         doc_copy(i).wait_recv()
-        tile_into(s_far, q, k_far, i * K_CHUNK, 1, K_CHUNK)
+        part = pl.ds(pl.multiple_of(i * K_CHUNK, K_CHUNK), K_CHUNK)
+        s_far[...] += logit_scale * lax.dot_general(
+            q[:, part], k_far[:, part], (((1,), (1,)), ((), ())), preferred_element_type=jnp.float32
+        )
 
     far_top, far_total = row_partial([s_far])
     near_top = row_top[:, 0:1]
@@ -226,7 +248,12 @@
         dk_store(i).start()
 
     for i in range(K_COUNT):
-        doc_copy(i).wait_send()
+        if i != AHEAD:
+            doc_copy(i).wait_send()
+
+    @pl.when(core == 1)
+    def _():
+        doc_copy(AHEAD).wait_send()
 
     @pl.loop(0, P_COUNT)
     def _(i):
@@ -299,7 +326,8 @@
         + [
             pltpu.SemaphoreType.DMA((n,))
             for n in (3, K_COUNT, K_COUNT, 2, 2, 4, 4, P_COUNT, P_COUNT, 4, P_COUNT)
-        ],
+        ]
+        + [pltpu.SemaphoreType.REGULAR],
         compiler_params=pltpu.CompilerParams(
             collective_id=0, has_side_effects=True, vmem_limit_bytes=60 << 20
         ),

time: 188 us -> 188 us (level)
  no operation moved by 1% of the time
where the time goes in v4:
time: 188 us
  Pallas kernels  176 us (94%)
  waiting for transfers between devices  8.63 us (5%)
  starting transfers between devices  2.83 us (2%)
    pallas_call x1, Pallas kernels, shards(): pl.pallas_call(exchange, out_shape=(big, out((HEAD, D), bf16), out((LAST,...  169 us
    ppermute x1, waiting for transfers between devices, shards(): share = lax.ppermute(share_tail, ('grp', 'dev'), route)  8.63 us
    pallas_call x1, Pallas kernels, shards(): pl.pallas_call(settle, out_shape=(big, big, vector, vector), in_specs=[an...  6.54 us
  transfers between devices with their start and end apart: 1, of which 1 were waited for; matrix products, arithmetic and copies ran while one was open for 0% of the time, Pallas kernels for 3%

profile of v4, /device:TPU:1, one launch (start us, length us, event | category | flops | bytes accessed | tf_op | source)
XLA Modules:
  0.0 188.3 jit_solution(1350358418504475765)
XLA Ops:
  0.6 168.5 %shard_map.66 = (bf16[512,4096]{1,0:T(8,128)(2,1)}, bf16[384,4096]{1,0:T(8,128)(2,1)}, bf16[128,4096]{1,0:T(8,128)(2,1)}, f32[128,4096]{1,0:T(8,128)}, f32[8,512]{1,0:T(8,128)}) custom-call(bf16[512,4096]{1,0:T(8,128)(2,1)} %q_hbm.1, bf16[512,4096]{1,0:T(8,128)(2,1)} %k_hbm.1, s32[1,512]{1,0:T(1,128)} %pair_hbm.1), custom_call_target="tpu_custom_call" | custom-call | flops 21474836480 | bytes 33554432 | tf_op jit(solution)/shard_map/pallas_call | solution.py:313
  169.2 0.0 copy-start
  169.2 2.8 %collective-permute-start = (bf16[128,4096]{1,0:T(8,128)(2,1)}, bf16[128,4096]{1,0:T(8,128)(2,1)S(1)}, u32[]{:S(2)}, u32[]{:S(2)}) collective-permute-start(bf16[128,4096]{1,0:T(8,128)(2,1)} %get-tuple-element.18), channel_id=1, source_target_pairs={{0,16},{1,17},{2,18},{3,19},{4,20},{5,21},{6,22},{7,23},{8,24},{9,... | collective-permute-start | bytes 3145736 | tf_op jit(solution)/shard_map/ppermute | solution.py:340
  172.0 6.5 %shard_map.67 = (bf16[512,4096]{1,0:T(8,128)(2,1)}, bf16[512,4096]{1,0:T(8,128)(2,1)}, f32[512]{0:T(512)}, f32[512]{0:T(512)}) custom-call(bf16[512,4096]{1,0:T(8,128)(2,1)} %get-tuple-element.13.dq_in, bf16[384,4096]{1,0:T(8,128)(2,1)} %get-tuple-element.14.dk_in, f32[8,512]{1,0:T(8,128)} %get-tuple-element.15.loss_in), custom_call_target="tpu_custom_call" | custom-call | bytes 16777216 | tf_op jit(solution)/shard_map/pallas_call | solution.py:342
  178.6 8.6 %collective-permute-done.share = bf16[128,4096]{1,0:T(8,128)(2,1)S(1)} collective-permute-done((bf16[128,4096]{1,0:T(8,128)(2,1)}, bf16[128,4096]{1,0:T(8,128)(2,1)S(1)}, u32[]{:S(2)}, u32[]{:S(2)}) %collective-permute-start) | collective-permute-done | bytes 1048608 | tf_op jit(solution)/shard_map/ppermute | solution.py:340
  187.2 0.0 copy-done
  187.2 1.1 shard_map.68
Async XLA Ops:
  169.2 18.0 %copy-start = (f32[128,4096]{1,0:T(8,128)S(1)}, f32[128,4096]{1,0:T(8,128)}, u32[]{:S(2)}) copy-start(f32[128,4096]{1,0:T(8,128)} %get-tuple-element.17.acc) | copy-start | bytes 6291460
  169.2 18.0 %collective-permute-start = (bf16[128,4096]{1,0:T(8,128)(2,1)}, bf16[128,4096]{1,0:T(8,128)(2,1)S(1)}, u32[]{:S(2)}, u32[]{:S(2)}) collective-permute-start(bf16[128,4096]{1,0:T(8,128)(2,1)} %get-tuple-element.18), channel_id=1, source_target_pairs={{0,16},{1,17},{2,18},{3,19},{4,20},{5,21},{6,22},{7,23},{8,24},{9,... | collective-permute-start | bytes 3145736 | tf_op jit(solution)/shard_map/ppermute | solution.py:340
